TPU v7x, 256 devices: a whole 4x4x8 slice. The times are simulated.
256 devices in a mesh: section: 32 (over z_lo, y, core), expert: 8 (over x, z_hi).
Axes of the slice: x: 4, y: 4, z: 8 (z_hi: 2, z_lo: 4; z = z_hi * 4 + z_lo), core: 2. Of those that a mesh axis runs over, the one named last changes fastest.
Arguments:
- forward_in: bfloat16 [32, 512, 7168], P('section', 'expert'), may hold values from -6 to 6
- entering: bfloat16 [1, 512, 7168], P(None, 'expert'), may hold values from -6 to 6
- cotangent_in: bfloat16 [32, 512, 7168], P('section', 'expert'), may hold values from -6 to 6
- cot_entering: bfloat16 [1, 512, 7168], P(None, 'expert'), may hold values from -6 to 6
- stash: bfloat16 [2, 32, 512, 7168], P(None, 'section', 'expert'), may hold values from -6 to 6
- norm_gain: float32 [32, 7168], P('section'), may hold values from 0.5 to 1.5
- w_gate: bfloat16 [32, 1, 7168, 1024], P('section', None, None, 'expert'), may hold values from -0.0625 to 0.0625
- w_up: bfloat16 [32, 1, 7168, 1024], P('section', None, None, 'expert'), may hold values from -0.0625 to 0.0625
- w_down: bfloat16 [32, 1, 1024, 7168], P('section', None, 'expert'), may hold values from -0.1875 to 0.1875
- ids_fwd: int32 [2, 32, 512, 8], P(None, 'section'), may hold values from 0 to 255, as said below
- route_fwd: float32 [2, 32, 512, 8], P(None, 'section'), may hold values from 0.25 to 1.5
- ids_bwd: int32 [2, 32, 512, 8], P(None, 'section'), may hold values from 0 to 255, as said below
- route_bwd: float32 [2, 32, 512, 8], P(None, 'section'), may hold values from 0.25 to 1.5
Outputs:
- forward_out: bfloat16 [32, 512, 7168], P('section', 'expert')
- cotangent_out: bfloat16 [32, 512, 7168], P('section', 'expert')
Inputs may be any that keep to these rules, and one draw needn't show every extreme that they name: `ids_fwd`: each row names 8 different experts. Among the 64 rows of one index of expert (aligned blocks of the token dimension), from 1 to 16 rows name any one expert below 1; for each such expert some step and layer have exactly 16 such rows on every index of expert. `ids_bwd`: as for ids_fwd.
All inputs are finite; a program needn't handle non-finite values.
Results may differ from a plain program's by a relative error of at most 0.006.
Values may be sent and summed in bfloat16 or wider, within the bound.
No kernel may reach another device: no remote copies, remote signals or barrier semaphores. Data moves between devices by JAX's collectives and lax.ppermute only.
A program may use at most 128 MiB of HBM per device.

v0:
```python
import jax
import jax.numpy as jnp
from jax import lax
from jax.sharding import PartitionSpec as P

CAP = 16
EPSILON = 1e-06


def from_behind(block, axis, distance):
    devices = range(lax.axis_size(axis))
    route = [(i - distance, i) for i in devices if i - distance in devices]
    return lax.ppermute(block, axis, route)


def routing_plan(ids, weights, flight, groups, capacity, own_index):
    experts = jnp.arange(flight, dtype=jnp.int32)
    matches = (ids[:, :, None] == experts[None, None, :]).astype(jnp.float32)
    mixing = jnp.sum(weights[:, :, None] * matches, axis=1)
    member = (jnp.sum(matches, axis=1) > 0).astype(jnp.int32).reshape(groups, -1, flight)
    slot_of = jnp.cumsum(member, axis=1) - 1
    slot_ids = jnp.arange(capacity, dtype=jnp.int32)
    one_hot = ((member[..., None] == 1) & (slot_of[..., None] == slot_ids)).astype(jnp.float32)
    pack_all = jnp.transpose(one_hot, (2, 0, 3, 1))
    mix_blocks = jnp.transpose(mixing.reshape(groups, -1, flight), (2, 0, 1))
    slot_weight = jnp.sum(pack_all * mix_blocks[:, :, None, :], axis=3)
    own_pack = lax.dynamic_index_in_dim(pack_all, own_index, 1, keepdims=False)
    return (own_pack, slot_weight.reshape(flight, groups * capacity))


def pack_rows(own_pack, source):
    return jnp.einsum(
        "ect,td->ecd", own_pack.astype(jnp.bfloat16), source, preferred_element_type=jnp.float32
    ).astype(jnp.bfloat16)


def unpack_rows(own_pack, summed):
    return jnp.einsum(
        "ect,ecd->td",
        own_pack,
        summed,
        precision=lax.Precision.HIGHEST,
        preferred_element_type=jnp.float32,
    )


def norm_pieces(source, norm_scale):
    row_floats = source.astype(jnp.float32)
    inverse_root_square = lax.rsqrt(
        jnp.mean(row_floats * row_floats, axis=-1, keepdims=True) + EPSILON
    )
    centered_input = row_floats * inverse_root_square
    return ((centered_input * norm_scale).astype(jnp.bfloat16), centered_input, inverse_root_square)


def expert_forward(packed, gate_dev, up_dev, down_dev, slot_weight):
    gate_pre = jnp.einsum("erd,edf->erf", packed, gate_dev, preferred_element_type=jnp.float32)
    up_pre = jnp.einsum("erd,edf->erf", packed, up_dev, preferred_element_type=jnp.float32)
    hidden = (gate_pre * jax.nn.sigmoid(gate_pre) * up_pre).astype(jnp.bfloat16)
    outputs = jnp.einsum("erf,efd->erd", hidden, down_dev, preferred_element_type=jnp.float32)
    return slot_weight[:, :, None] * outputs


def expert_backward(packed, cot_packed, gate_dev, up_dev, down_dev, slot_weight):
    gate_pre = jnp.einsum("erd,edf->erf", packed, gate_dev, preferred_element_type=jnp.float32)
    up_pre = jnp.einsum("erd,edf->erf", packed, up_dev, preferred_element_type=jnp.float32)
    sigma = jax.nn.sigmoid(gate_pre)
    activated = gate_pre * sigma
    expert_cot = (slot_weight[:, :, None] * cot_packed.astype(jnp.float32)).astype(jnp.bfloat16)
    hidden_cot = jnp.einsum(
        "erd,efd->erf", expert_cot, down_dev, preferred_element_type=jnp.float32
    )
    gate_cot = (hidden_cot * up_pre * sigma * (1.0 + gate_pre * (1.0 - sigma))).astype(jnp.bfloat16)
    up_cot = (hidden_cot * activated).astype(jnp.bfloat16)
    partial_cot = jnp.einsum("erf,edf->erd", gate_cot, gate_dev, preferred_element_type=jnp.float32)
    return partial_cot + jnp.einsum(
        "erf,edf->erd", up_cot, up_dev, preferred_element_type=jnp.float32
    )


def on_device(
    forward_in,
    entering,
    cotangent_in,
    cot_entering,
    stash,
    norm_gain,
    w_gate,
    w_up,
    w_down,
    ids_fwd,
    route_fwd,
    ids_bwd,
    route_bwd,
):
    section_index = lax.axis_index("section")
    last_section = lax.axis_size("section") - 1
    groups = lax.axis_size("expert")
    own_index = lax.axis_index("expert")
    scale_row_vector = norm_gain[0]
    gate_dev = w_gate[0]
    up_dev = w_up[0]
    down_dev = w_down[0]
    flight = gate_dev.shape[0]
    step_count = stash.shape[0]
    forward_token_rows = forward_in[0]
    cot_rows = cotangent_in[0]
    next_fwd = forward_token_rows
    next_cot = cot_rows
    for tick_index in range(step_count):
        own_fwd, weight_fwd = routing_plan(
            ids_fwd[tick_index, 0], route_fwd[tick_index, 0], flight, groups, CAP, own_index
        )
        own_bwd, weight_bwd = routing_plan(
            ids_bwd[tick_index, 0], route_bwd[tick_index, 0], flight, groups, CAP, own_index
        )
        normalized_forward, centered_forward, root_square_forward = norm_pieces(
            forward_token_rows, scale_row_vector
        )
        normalized_backward, centered_backward, root_square_backward = norm_pieces(
            stash[tick_index, 0], scale_row_vector
        )
        packed_fwd = pack_rows(own_fwd, normalized_forward)
        packed_bwd = pack_rows(own_bwd, normalized_backward)
        packed_cot = pack_rows(own_bwd, cot_rows)
        whole_fwd, whole_bwd, whole_cot = (
            lax.all_gather(packed_fwd, "expert", axis=1, tiled=True),
            lax.all_gather(packed_bwd, "expert", axis=1, tiled=True),
            lax.all_gather(packed_cot, "expert", axis=1, tiled=True),
        )
        partial_fwd = expert_forward(whole_fwd, gate_dev, up_dev, down_dev, weight_fwd)
        partial_bwd = expert_backward(whole_bwd, whole_cot, gate_dev, up_dev, down_dev, weight_bwd)
        sum_fwd, sum_bwd = (
            lax.psum_scatter(partial_fwd, "expert", scatter_dimension=1, tiled=True),
            lax.psum_scatter(partial_bwd, "expert", scatter_dimension=1, tiled=True),
        )
        next_fwd = (forward_token_rows.astype(jnp.float32) + unpack_rows(own_fwd, sum_fwd)).astype(
            jnp.bfloat16
        )
        scaled_rows = unpack_rows(own_bwd, sum_bwd) * scale_row_vector
        next_cot = cot_rows.astype(jnp.float32) + root_square_backward * (
            scaled_rows
            - centered_backward * jnp.mean(scaled_rows * centered_backward, axis=-1, keepdims=True)
        )
        next_cot = next_cot.astype(jnp.bfloat16)
        if tick_index + 1 < step_count:
            moved_fwd = from_behind(next_fwd, "section", 1)
            moved_cot = from_behind(next_cot, "section", -1)
            forward_token_rows = jnp.where(section_index == 0, entering[tick_index], moved_fwd)
            cot_rows = jnp.where(section_index == last_section, cot_entering[tick_index], moved_cot)
    return (next_fwd[None], next_cot[None])


def solution(mesh):
    placed = (
        P("section", "expert", None),
        P(None, "expert", None),
        P("section", "expert", None),
        P(None, "expert", None),
        P(None, "section", "expert", None),
        P("section", None),
        P("section", None, None, "expert"),
        P("section", None, None, "expert"),
        P("section", None, "expert", None),
        P(None, "section", None, None),
        P(None, "section", None, None),
        P(None, "section", None, None),
        P(None, "section", None, None),
    )
    return jax.shard_map(
        on_device,
        mesh=mesh,
        in_specs=placed,
        out_specs=(P("section", "expert", None), P("section", "expert", None)),
        check_vma=False,
    )
```

profile of v0, /device:TPU:8, one launch (start us, length us, event | category | flops | bytes accessed | tf_op | source)
XLA Modules:
  0.0 941.1 jit_solution(7283005679157287276)
XLA Ops:
  18.7 70.1 %all-gather.19.cloned.1.call-done = bf16[128,7168]{1,0:T(8,128)(2,1)} async-done(((bf16[16,7168]{1,0:T(8,128)(2,1)}), bf16[128,7168]{1,0:T(8,128)(2,1)}) %all-gather.19.cloned.1.call-update) | async-done | bytes 1835024 | tf_op jit(solution)/shard_map/all_gather | solution.py:128
  91.5 68.7 %all-gather.17.cloned.1.call-done = bf16[128,7168]{1,0:T(8,128)(2,1)} async-done(((bf16[16,7168]{1,0:T(8,128)(2,1)}), bf16[128,7168]{1,0:T(8,128)(2,1)}) %all-gather.17.cloned.1.call-update) | async-done | bytes 1835024 | tf_op jit(solution)/shard_map/all_gather | solution.py:129
  163.0 5.1 fusion.66
  168.1 4.5 fusion.1
  172.9 58.7 %all-gather.13.cloned.1.call-done = bf16[128,7168]{1,0:T(8,128)(2,1)} async-done(((bf16[16,7168]{1,0:T(8,128)(2,1)}), bf16[128,7168]{1,0:T(8,128)(2,1)}) %all-gather.13.cloned.1.call-update) | async-done | bytes 1835024 | tf_op jit(solution)/shard_map/all_gather | solution.py:127
  234.3 5.1 fusion.3
  239.8 112.7 %reduce-scatter.9.cloned.1.call-done = f32[1,16,7168]{2,1,0:T(8,128)} async-done(((f32[1,128,7168]{2,1,0:T(8,128)}), f32[1,16,7168]{2,1,0:T(8,128)}) %reduce-scatter.9.cloned.1.call-update) | async-done | bytes 458768 | tf_op jit(solution)/shard_map/reduce_scatter | solution.py:135
  352.5 4.4 fusion.34
  358.0 3.5 fusion.27
  363.5 11.2 %collective-permute-done.1 = bf16[64,7168]{1,0:T(8,128)(2,1)} collective-permute-done((bf16[64,7168]{1,0:T(8,128)(2,1)}, bf16[64,7168]{1,0:T(8,128)(2,1)}, u32[]{:S(2)}, u32[]{:S(2)}) %collective-permute-start.1) | collective-permute-done | bytes 917536 | tf_op jit(solution)/shard_map/ppermute | solution.py:13
  377.0 95.4 %reduce-scatter.5.cloned.1.call-done = f32[1,16,7168]{2,1,0:T(8,128)} async-done(((f32[1,128,7168]{2,1,0:T(8,128)}), f32[1,16,7168]{2,1,0:T(8,128)}) %reduce-scatter.5.cloned.1.call-update) | async-done | bytes 458768 | tf_op jit(solution)/shard_map/reduce_scatter | solution.py:134
  472.3 3.2 fusion.4
  477.8 12.8 %collective-permute-done = bf16[64,7168]{1,0:T(8,128)(2,1)} collective-permute-done((bf16[64,7168]{1,0:T(8,128)(2,1)}, bf16[64,7168]{1,0:T(8,128)(2,1)}, u32[]{:S(2)}, u32[]{:S(2)}) %collective-permute-start) | collective-permute-done | bytes 917536 | tf_op jit(solution)/shard_map/ppermute | solution.py:13
  495.0 48.2 %all-gather.23.cloned.1.call-done = bf16[128,7168]{1,0:T(8,128)(2,1)} async-done(((bf16[16,7168]{1,0:T(8,128)(2,1)}), bf16[128,7168]{1,0:T(8,128)(2,1)}) %all-gather.23.cloned.1.call-update) | async-done | bytes 1835024 | tf_op jit(solution)/shard_map/all_gather | solution.py:128
  545.9 68.1 %all-gather.21.cloned.1.call-done = bf16[128,7168]{1,0:T(8,128)(2,1)} async-done(((bf16[16,7168]{1,0:T(8,128)(2,1)}), bf16[128,7168]{1,0:T(8,128)(2,1)}) %all-gather.21.cloned.1.call-update) | async-done | bytes 1835024 | tf_op jit(solution)/shard_map/all_gather | solution.py:129
  616.8 5.1 fusion.62
  621.9 4.5 fusion
  626.7 58.7 %all-gather.15.cloned.1.call-done = bf16[128,7168]{1,0:T(8,128)(2,1)} async-done(((bf16[16,7168]{1,0:T(8,128)(2,1)}), bf16[128,7168]{1,0:T(8,128)(2,1)}) %all-gather.15.cloned.1.call-update) | async-done | bytes 1835024 | tf_op jit(solution)/shard_map/all_gather | solution.py:127
  688.1 5.1 fusion.2
  693.2 113.2 %reduce-scatter.11.cloned.1.call-done = f32[1,16,7168]{2,1,0:T(8,128)} async-done(((f32[1,128,7168]{2,1,0:T(8,128)}), f32[1,16,7168]{2,1,0:T(8,128)}) %reduce-scatter.11.cloned.1.call-update) | async-done | bytes 458768 | tf_op jit(solution)/shard_map/reduce_scatter | solution.py:135
  806.4 3.8 fusion.18
  810.2 117.5 %reduce-scatter.7.cloned.1.call-done = f32[1,16,7168]{2,1,0:T(8,128)} async-done(((f32[1,128,7168]{2,1,0:T(8,128)}), f32[1,16,7168]{2,1,0:T(8,128)}) %reduce-scatter.7.cloned.1.call-update) | async-done | bytes 458768 | tf_op jit(solution)/shard_map/reduce_scatter | solution.py:134
  927.7 3.3 fusion.6
  931.0 3.3 fusion.123
  (99 shorter events, 40.4 us)
Async XLA Ops:
  7.2 155.8 %copy-start = (bf16[1,1,7168,128]{3,2,1,0:T(8,128)(2,1)S(1)}, bf16[1,1,7168,128]{3,2,1,0:T(8,128)(2,1)}, u32[]{:S(2)}) copy-start(bf16[1,1,7168,128]{3,2,1,0:T(8,128)(2,1)} %param.20) | copy-start | bytes 5505028
  7.2 6.0 copy-start.4
  7.2 81.6 %all-gather.19.cloned.1.call-start = ((), (), s32[]{:S(2)}) async-start(), calls=%async_computation.11 | async-start | bytes 2064384 | tf_op jit(solution)/shard_map/all_gather | solution.py:128
  10.7 3.5 copy-start.6
  10.7 3.5 copy-start.7
  10.8 5.3 copy-start.8
  13.1 147.1 %all-gather.17.cloned.1.call-start = ((), (), s32[]{:S(2)}) async-start(), calls=%async_computation.10 | async-start | bytes 2064384 | tf_op jit(solution)/shard_map/all_gather | solution.py:129
  14.1 217.5 %all-gather.13.cloned.1.call-start = ((), (), s32[]{:S(2)}) async-start(), calls=%async_computation.8 | async-start | bytes 2064384 | tf_op jit(solution)/shard_map/all_gather | solution.py:127
  18.4 334.1 %reduce-scatter.9.cloned.1.call-start = ((), (), s32[]{:S(2)}) async-start(), calls=%async_computation.6 | async-start | bytes 4128768 | tf_op jit(solution)/shard_map/reduce_scatter | solution.py:135
  172.6 299.7 %reduce-scatter.5.cloned.1.call-start = ((), (), s32[]{:S(2)}) async-start(), calls=%async_computation.4 | async-start | bytes 4128768 | tf_op jit(solution)/shard_map/reduce_scatter | solution.py:134
  239.4 303.8 %all-gather.23.cloned.1.call-start = ((), (), s32[]{:S(2)}) async-start(), calls=%async_computation.13 | async-start | bytes 2064384 | tf_op jit(solution)/shard_map/all_gather | solution.py:128
  352.5 4.4 copy-start.1
  358.0 256.0 %all-gather.21.cloned.1.call-start = ((), (), s32[]{:S(2)}) async-start(), calls=%async_computation.12 | async-start | bytes 2064384 | tf_op jit(solution)/shard_map/all_gather | solution.py:129
  358.0 16.7 %copy-start.3 = (bf16[1,64,7168]{2,1,0:T(8,128)(2,1)S(1)}, bf16[1,64,7168]{2,1,0:T(8,128)(2,1)}, u32[]{:S(2)}) copy-start(bf16[1,64,7168]{2,1,0:T(8,128)(2,1)} %param.16) | copy-start | bytes 2752516
  361.6 13.1 %collective-permute-start.1 = (bf16[64,7168]{1,0:T(8,128)(2,1)}, bf16[64,7168]{1,0:T(8,128)(2,1)}, u32[]{:S(2)}, u32[]{:S(2)}) collective-permute-start(bf16[64,7168]{1,0:T(8,128)(2,1)} %fusion.27), channel_id=1, source_target_pairs={{8,0},{16,8},{24,16},{32,24},{40,32},{48,40},{56,48},{64,56},{72,6... | collective-permute-start | bytes 2752520 | tf_op jit(solution)/shard_map/ppermute | solution.py:13
  376.9 308.5 %all-gather.15.cloned.1.call-start = ((), (), s32[]{:S(2)}) async-start(), calls=%async_computation.9 | async-start | bytes 2064384 | tf_op jit(solution)/shard_map/all_gather | solution.py:127
  475.5 15.0 %collective-permute-start = (bf16[64,7168]{1,0:T(8,128)(2,1)}, bf16[64,7168]{1,0:T(8,128)(2,1)}, u32[]{:S(2)}, u32[]{:S(2)}) collective-permute-start(bf16[64,7168]{1,0:T(8,128)(2,1)} %fusion.4), channel_id=1, source_target_pairs={{0,8},{8,16},{16,24},{24,32},{32,40},{40,48},{48,56},{56,64},{64,7... | collective-permute-start | bytes 2752520 | tf_op jit(solution)/shard_map/ppermute | solution.py:13
  492.4 0.9 copy-start.5
  494.5 311.9 %reduce-scatter.11.cloned.1.call-start = ((), (), s32[]{:S(2)}) async-start(), calls=%async_computation.7 | async-start | bytes 4128768 | tf_op jit(solution)/shard_map/reduce_scatter | solution.py:135
  626.4 301.3 %reduce-scatter.7.cloned.1.call-start = ((), (), s32[]{:S(2)}) async-start(), calls=%async_computation.5 | async-start | bytes 4128768 | tf_op jit(solution)/shard_map/reduce_scatter | solution.py:134
  927.7 3.3 copy-start.2
Sparse Core Ops, SparseCore 0:
  13.2 75.5 all-gather.18
  92.0 68.1 all-gather.16
  163.4 68.1 all-gather.12
  235.7 116.6 reduce-scatter.8
  357.2 115.1 reduce-scatter.4
  474.8 68.3 all-gather.22
  545.8 68.1 all-gather.20
  617.2 68.1 all-gather.14
  689.7 116.6 reduce-scatter.10
  811.1 116.5 reduce-scatter.6
where the time goes:
time: 942 us; the launch traced here: 941 us
  waiting for transfers between devices  836 us (89%)
  matrix products  70.1 us (7%)
  other arithmetic  14.7 us (2%)
  between operations  14.5 us (2%)
    reduce_scatter x2, waiting for transfers between devices, on_device(): lax.psum_scatter(partial_bwd, 'expert', scatter_dimension=1, tiled=True)  226 us
    reduce_scatter x2, waiting for transfers between devices, on_device(): lax.psum_scatter(partial_fwd, 'expert', scatter_dimension=1, tiled=True)  213 us
    all_gather x2, waiting for transfers between devices, on_device(): lax.all_gather(packed_cot, 'expert', axis=1, tiled=True)  137 us
    all_gather x2, waiting for transfers between devices, on_device(): lax.all_gather(packed_bwd, 'expert', axis=1, tiled=True)  118 us
    all_gather x2, waiting for transfers between devices, on_device(): lax.all_gather(packed_fwd, 'expert', axis=1, tiled=True)  117 us
    ppermute x2, waiting for transfers between devices, from_behind(): return lax.ppermute(block, axis, route)  24 us
  transfers between devices with their start and end apart: 12, of which 12 were waited for; matrix products, arithmetic and copies ran while one was open for 8% of the time, Pallas kernels for 0%

commit v1 on v0

--- a/solution.py
+++ b/solution.py
@@ -124,7 +124,10 @@
         packed_bwd = pack_rows(own_bwd, normalized_backward)
         packed_cot = pack_rows(own_bwd, cot_rows)
         whole_fwd, whole_bwd, whole_cot = (
-            lax.all_gather(packed_fwd, "expert", axis=1, tiled=True),
+            jnp.concatenate(
+                lax.all_to_all(jnp.stack(lax.axis_size("expert") * [packed_fwd]), "expert", 0, 0),
+                axis=1,
+            ),
             lax.all_gather(packed_bwd, "expert", axis=1, tiled=True),
             lax.all_gather(packed_cot, "expert", axis=1, tiled=True),
         )

time: 942 us -> 860 us (0.913)
  waiting for transfers between devices: 836 us -> 745 us
    all_gather x2 -> x0, waiting for transfers between devices: 117 us -> none  [on_device(): lax.all_gather(packed_fwd, 'expert', axis=1, tiled=True)]
    all_to_all x0 -> x2, waiting for transfers between devices: none -> 104 us  [on_device(): lax.all_to_all(jnp.stack(lax.axis_size('expert') * [packed_fwd]), 'expert...]
    all_gather x2, waiting for transfers between devices: 118 us -> 74.3 us  [on_device(): lax.all_gather(packed_bwd, 'expert', axis=1, tiled=True)]
    reduce_scatter x2, waiting for transfers between devices: 226 us -> 186 us  [on_device(): lax.psum_scatter(partial_bwd, 'expert', scatter_dimension=1, tiled=True)]
    reduce_scatter x2, waiting for transfers between devices: 213 us -> 226 us  [on_device(): lax.psum_scatter(partial_fwd, 'expert', scatter_dimension=1, tiled=True)]
  transfers between devices with their start and end apart: 12 -> 12, of which waited for: 12 -> 11; matrix products, arithmetic and copies ran while one was open for 8% -> 6% of each run, Pallas kernels for 0% -> 0%
where the time goes in v1:
time: 860 us
  waiting for transfers between devices  745 us (87%)
  matrix products  67.5 us (8%)
  between operations  14.5 us (2%)
  other arithmetic  14.4 us (2%)
  starting transfers between devices  13.1 us (2%)
    reduce_scatter x2, waiting for transfers between devices, on_device(): lax.psum_scatter(partial_fwd, 'expert', scatter_dimension=1, tiled=True)  226 us
    reduce_scatter x2, waiting for transfers between devices, on_device(): lax.psum_scatter(partial_bwd, 'expert', scatter_dimension=1, tiled=True)  186 us
    all_gather x2, waiting for transfers between devices, on_device(): lax.all_gather(packed_cot, 'expert', axis=1, tiled=True)  138 us
    all_to_all x2, waiting for transfers between devices, on_device(): lax.all_to_all(jnp.stack(lax.axis_size('expert') * [packed_fwd]), 'expert...  104 us
    all_gather x2, waiting for transfers between devices, on_device(): lax.all_gather(packed_bwd, 'expert', axis=1, tiled=True)  74.3 us
    ppermute x2, waiting for transfers between devices, from_behind(): return lax.ppermute(block, axis, route)  17.6 us
  transfers between devices with their start and end apart: 12, of which 11 were waited for; matrix products, arithmetic and copies ran while one was open for 6% of the time, Pallas kernels for 0%

profile of v1, /device:TPU:8, one launch (start us, length us, event | category | flops | bytes accessed | tf_op | source)
XLA Modules:
  0.0 859.6 jit_solution(6427437001944587585)
XLA Ops:
  14.4 74.3 %all-gather.11.cloned.1.call-done = bf16[128,7168]{1,0:T(8,128)(2,1)} async-done(((bf16[16,7168]{1,0:T(8,128)(2,1)}), bf16[128,7168]{1,0:T(8,128)(2,1)}) %all-gather.11.cloned.1.call-update) | async-done | bytes 1835024 | tf_op jit(solution)/shard_map/all_gather | solution.py:131
  91.4 68.7 %all-gather.9.cloned.1.call-done = bf16[128,7168]{1,0:T(8,128)(2,1)} async-done(((bf16[16,7168]{1,0:T(8,128)(2,1)}), bf16[128,7168]{1,0:T(8,128)(2,1)}) %all-gather.9.cloned.1.call-update) | async-done | bytes 1835024 | tf_op jit(solution)/shard_map/all_gather | solution.py:132
  162.9 5.1 fusion.66
  168.0 4.5 fusion.1
  175.1 114.2 %reduce-scatter.9.cloned.1.call-done = f32[1,16,7168]{2,1,0:T(8,128)} async-done(((f32[1,128,7168]{2,1,0:T(8,128)}), f32[1,16,7168]{2,1,0:T(8,128)}) %reduce-scatter.9.cloned.1.call-update) | async-done | bytes 458768 | tf_op jit(solution)/shard_map/reduce_scatter | solution.py:138
  289.3 4.4 fusion.34
  294.8 3.2 fusion.27
  301.9 4.5 all-to-all-start
  306.4 4.8 collective-permute-done.1
  313.7 61.6 %all-to-all-done = bf16[8,1,16,7168]{3,2,1,0:T(8,128)(2,1)} async-done(((bf16[8,1,16,7168]{3,2,1,0:T(8,128)(2,1)}), bf16[8,1,16,7168]{3,2,1,0:T(8,128)(2,1)}, u32[]{:S(2)}, u32[]{:S(2)}) %all-to-all-start) | async-done | bytes 1835040 | tf_op jit(solution)/shard_map/all_to_all | solution.py:128
  378.0 5.1 fusion.3
  386.3 69.1 %all-gather.13.cloned.1.call-done = bf16[128,7168]{1,0:T(8,128)(2,1)} async-done(((bf16[16,7168]{1,0:T(8,128)(2,1)}), bf16[128,7168]{1,0:T(8,128)(2,1)}) %all-gather.13.cloned.1.call-update) | async-done | bytes 1835024 | tf_op jit(solution)/shard_map/all_gather | solution.py:132
  458.2 5.0 fusion.62
  463.2 4.5 fusion
  467.7 109.1 %reduce-scatter.5.cloned.1.call-done = f32[1,16,7168]{2,1,0:T(8,128)} async-done(((f32[1,128,7168]{2,1,0:T(8,128)}), f32[1,16,7168]{2,1,0:T(8,128)}) %reduce-scatter.5.cloned.1.call-update) | async-done | bytes 458768 | tf_op jit(solution)/shard_map/reduce_scatter | solution.py:137
  582.2 12.8 %collective-permute-done = bf16[64,7168]{1,0:T(8,128)(2,1)} collective-permute-done((bf16[64,7168]{1,0:T(8,128)(2,1)}, bf16[64,7168]{1,0:T(8,128)(2,1)}, u32[]{:S(2)}, u32[]{:S(2)}) %collective-permute-start) | collective-permute-done | bytes 917536 | tf_op jit(solution)/shard_map/ppermute | solution.py:13
  599.7 4.3 all-to-all-start.1
  604.3 42.3 %all-to-all-done.1 = bf16[8,1,16,7168]{3,2,1,0:T(8,128)(2,1)} async-done(((bf16[8,1,16,7168]{3,2,1,0:T(8,128)(2,1)}), bf16[8,1,16,7168]{3,2,1,0:T(8,128)(2,1)}, u32[]{:S(2)}, u32[]{:S(2)}) %all-to-all-start.1) | async-done | bytes 1835040 | tf_op jit(solution)/shard_map/all_to_all | solution.py:128
  649.2 5.1 fusion.2
  654.4 71.5 %reduce-scatter.11.cloned.1.call-done = f32[1,16,7168]{2,1,0:T(8,128)} async-done(((f32[1,128,7168]{2,1,0:T(8,128)}), f32[1,16,7168]{2,1,0:T(8,128)}) %reduce-scatter.11.cloned.1.call-update) | async-done | bytes 458768 | tf_op jit(solution)/shard_map/reduce_scatter | solution.py:138
  725.8 3.8 fusion.18
  729.7 116.5 %reduce-scatter.7.cloned.1.call-done = f32[1,16,7168]{2,1,0:T(8,128)} async-done(((f32[1,128,7168]{2,1,0:T(8,128)}), f32[1,16,7168]{2,1,0:T(8,128)}) %reduce-scatter.7.cloned.1.call-update) | async-done | bytes 458768 | tf_op jit(solution)/shard_map/reduce_scatter | solution.py:137
  846.1 3.3 fusion.6
  849.5 3.3 fusion.123
  (101 shorter events, 44.3 us)
Async XLA Ops:
  7.2 155.7 %copy-start = (bf16[1,1,7168,128]{3,2,1,0:T(8,128)(2,1)S(1)}, bf16[1,1,7168,128]{3,2,1,0:T(8,128)(2,1)}, u32[]{:S(2)}) copy-start(bf16[1,1,7168,128]{3,2,1,0:T(8,128)(2,1)} %param.20) | copy-start | bytes 5505028
  7.2 5.9 copy-start.4
  7.2 81.5 %all-gather.11.cloned.1.call-start = ((), (), s32[]{:S(2)}) async-start(), calls=%async_computation.11 | async-start | bytes 2064384 | tf_op jit(solution)/shard_map/all_gather | solution.py:131
  13.1 147.1 %all-gather.9.cloned.1.call-start = ((), (), s32[]{:S(2)}) async-start(), calls=%async_computation.10 | async-start | bytes 2064384 | tf_op jit(solution)/shard_map/all_gather | solution.py:132
  14.1 275.2 %reduce-scatter.9.cloned.1.call-start = ((), (), s32[]{:S(2)}) async-start(), calls=%async_computation.8 | async-start | bytes 4128768 | tf_op jit(solution)/shard_map/reduce_scatter | solution.py:138
  172.4 0.8 copy-start.7
  172.4 0.8 copy-start.8
  172.4 116.9 %copy-start.9 = (f32[1,7168]{1,0:T(1,128)S(1)}, f32[1,7168]{1,0:T(1,128)}, u32[]{:S(2)}) copy-start(f32[1,7168]{1,0:T(1,128)} %param.18) | copy-start | bytes 86020
  172.5 211.2 %all-gather.15.cloned.1.call-start = ((), (), s32[]{:S(2)}) async-start(), calls=%async_computation.13 | async-start | bytes 2064384 | tf_op jit(solution)/shard_map/all_gather | solution.py:131
  289.3 4.4 copy-start.1
  294.8 5.2 copy-start.5
  298.1 13.1 %collective-permute-start.1 = (bf16[64,7168]{1,0:T(8,128)(2,1)}, bf16[64,7168]{1,0:T(8,128)(2,1)}, u32[]{:S(2)}, u32[]{:S(2)}) collective-permute-start(bf16[64,7168]{1,0:T(8,128)(2,1)} %fusion.27), channel_id=1, source_target_pairs={{8,0},{16,8},{24,16},{32,24},{40,32},{48,40},{56,48},{64,56},{72,6... | collective-permute-start | bytes 2752520 | tf_op jit(solution)/shard_map/ppermute | solution.py:13
  301.9 9.3 %copy-start.3 = (bf16[1,64,7168]{2,1,0:T(8,128)(2,1)S(1)}, bf16[1,64,7168]{2,1,0:T(8,128)(2,1)}, u32[]{:S(2)}) copy-start(bf16[1,64,7168]{2,1,0:T(8,128)(2,1)} %param.16) | copy-start | bytes 2752516
  301.9 73.4 %all-to-all-start = ((bf16[8,1,16,7168]{3,2,1,0:T(8,128)(2,1)}), bf16[8,1,16,7168]{3,2,1,0:T(8,128)(2,1)}, u32[]{:S(2)}, u32[]{:S(2)}) async-start(bf16[8,1,16,7168]{3,2,1,0:T(8,128)(2,1)} %stack.4), calls=%async_computation | async-start | bytes 3670016 | tf_op jit(solution)/shard_map/all_to_all | solution.py:128
  306.4 149.1 %all-gather.13.cloned.1.call-start = ((), (), s32[]{:S(2)}) async-start(), calls=%async_computation.12 | async-start | bytes 2064384 | tf_op jit(solution)/shard_map/all_gather | solution.py:132
  313.4 263.3 %reduce-scatter.5.cloned.1.call-start = ((), (), s32[]{:S(2)}) async-start(), calls=%async_computation.6 | async-start | bytes 4128768 | tf_op jit(solution)/shard_map/reduce_scatter | solution.py:137
  383.2 342.7 %reduce-scatter.11.cloned.1.call-start = ((), (), s32[]{:S(2)}) async-start(), calls=%async_computation.9 | async-start | bytes 4128768 | tf_op jit(solution)/shard_map/reduce_scatter | solution.py:138
  580.0 15.0 %collective-permute-start = (bf16[64,7168]{1,0:T(8,128)(2,1)}, bf16[64,7168]{1,0:T(8,128)(2,1)}, u32[]{:S(2)}, u32[]{:S(2)}) collective-permute-start(bf16[64,7168]{1,0:T(8,128)(2,1)} %fusion.4), channel_id=1, source_target_pairs={{0,8},{8,16},{16,24},{24,32},{32,40},{40,48},{48,56},{56,64},{64,7... | collective-permute-start | bytes 2752520 | tf_op jit(solution)/shard_map/ppermute | solution.py:13
  596.9 0.9 copy-start.6
  599.7 46.9 %all-to-all-start.1 = ((bf16[8,1,16,7168]{3,2,1,0:T(8,128)(2,1)}), bf16[8,1,16,7168]{3,2,1,0:T(8,128)(2,1)}, u32[]{:S(2)}, u32[]{:S(2)}) async-start(bf16[8,1,16,7168]{3,2,1,0:T(8,128)(2,1)} %stack.5), calls=%async_computation.2 | async-start | bytes 3670016 | tf_op jit(solution)/shard_map/all_to_all | solution.py:128
  604.0 242.1 %reduce-scatter.7.cloned.1.call-start = ((), (), s32[]{:S(2)}) async-start(), calls=%async_computation.7 | async-start | bytes 4128768 | tf_op jit(solution)/shard_map/reduce_scatter | solution.py:137
  846.1 3.4 copy-start.2
Sparse Core Ops, SparseCore 0:
  13.2 75.4 all-gather.10
  91.9 68.2 all-gather.8
  172.6 116.6 reduce-scatter.8
  294.9 87.9 all-gather.14
  386.3 69.0 all-gather.12
  460.1 116.5 reduce-scatter.4
  581.0 144.7 reduce-scatter.10
  730.7 115.4 reduce-scatter.6
